TPU v7x, 256 devices: a whole 4x4x8 slice. The times are simulated.
256 devices in a mesh: wide: 64 (over z_hi, y, x, core), wall: 4 (over z_lo).
Axes of the slice: x: 4, y: 4, z: 8 (z_hi: 2, z_lo: 4; z = z_hi * 4 + z_lo), core: 2. Of those that a mesh axis runs over, the one named last changes fastest.
Arguments:
- source: float32 [32, 1024, 1024], P('wall', 'wide'), may hold values from -6 to 6
- spacing: float32 [32], replicated, may hold values from 0.5 to 2
Outputs:
- pressure: float32 [32, 1024, 1024], P('wall', 'wide')
All inputs are finite; a program needn't handle non-finite values.
Results may differ from a plain program's by a relative error of at most 0.0003.
Values sent between devices are 32-bit elements; how exact they have to be, the bound alone decides.
A program may use at most 64 MiB of HBM per device.

v0:
```python
import functools
import math

import jax
import jax.numpy as jnp
import ml_dtypes
import numpy as np
from jax import lax
from jax.experimental import pallas as pl
from jax.experimental.pallas import tpu as pltpu
from jax.sharding import PartitionSpec as P

MESH = pl.DeviceIdType.MESH
TWO_PI = 2.0 * math.pi
X = 1024
Z = 1024
ROWS = 32
WALL = 4
WIDE = 64
SLOTS = WALL * WIDE
ROWS_HERE = ROWS // WALL
SPAN_HERE = Z // WIDE
PIECE = 4


def split_pair(table):
    high = table.astype(ml_dtypes.bfloat16)
    low = (table - high.astype(np.float64)).astype(ml_dtypes.bfloat16)
    return high, low


@functools.cache
def tables():
    x = np.arange(X // 2)
    stream = []
    for parity in range(2):
        mode = 2 * np.arange(128)[:, None] + parity + 256 * np.arange(2)[None, :]
        angle = TWO_PI * ((mode[..., None] * x) % X) / X
        block = np.stack([np.cos(angle), -np.sin(angle)], axis=1)
        stream.append(block.reshape(512, 512))
    stream = np.concatenate(stream, axis=0)

    def complex_block(angle):
        cos, sin = np.cos(angle), np.sin(angle)
        return np.stack([np.stack([cos, sin], 1), np.stack([-sin, cos], 1)], 0)

    outer = np.arange(64)
    block = complex_block(TWO_PI * ((outer[:, None] * outer[None, :]) % 64) / 64)
    span_outer = np.einsum("parq,kl->pkaqrl", block, np.eye(2)).reshape(256, 256)
    inner = np.arange(16)
    block = complex_block(TWO_PI * ((inner[:, None] * inner[None, :]) % 16) / 16)
    span_inner = np.einsum("pbrl,yz->ypbrzl", block, np.eye(ROWS_HERE)).reshape(256, 256)
    angle = TWO_PI * (outer[:, None] * inner[None, :]) / Z
    angle = np.broadcast_to(angle[None, :, None, :], (2, 64, ROWS_HERE, 16)).reshape(128, 128)
    twist = np.stack([np.cos(angle), np.sin(angle), np.cos(angle).T, np.sin(angle).T])
    small = np.concatenate([span_outer, span_inner, span_inner.T, span_outer.T], axis=0)
    return split_pair(stream) + split_pair(small) + (twist.astype(np.float32),)


def deltas():
    steps = [
        (y, x, core, z)
        for y in range(4)
        for x in range(4)
        for core in range(2)
        for z in range(8)
        if (y, x, core, z) != (0, 0, 0, 0)
    ]
    hops = lambda d: min(d[0], 4 - d[0]) + min(d[1], 4 - d[1]) + min(d[3], 8 - d[3])
    return sorted(steps, key=lambda d: -hops(d))


def dot3(high, low, value, contract):
    dims = (contract, ((), ()))
    value_high = value.astype(jnp.bfloat16)
    value_low = (value - value_high.astype(jnp.float32)).astype(jnp.bfloat16)
    dot = functools.partial(lax.dot_general, dimension_numbers=dims, preferred_element_type=jnp.float32)
    return dot(high, value_high) + (dot(high, value_low) + dot(low, value_high))


NN = ((1,), (0,))
NT = ((1,), (1,))


def kernel(
    spacing, source, stream_high, stream_low, small_high, small_low, twist, out,
    send_a, recv_a, send_b, recv_b, gain, carry, pivot, work, solved,
    send_sem, recv_sem, own_sem,
):
    wide, wall = lax.axis_index("wide"), lax.axis_index("wall")
    slot = wall * WIDE + wide
    core = lax.rem(wide, 2)
    x = lax.rem(lax.div(wide, 2), 4)
    y = lax.rem(lax.div(wide, 8), 4)
    z = lax.div(wide, 32) * 4 + wall
    at_core = [lax.rem(core + d, 2) for d in range(2)]
    at_x = [lax.rem(x + d, 4) * 2 for d in range(4)]
    at_y = [lax.rem(y + d, 4) * 8 for d in range(4)]
    z_all = [lax.rem(z + d, 8) for d in range(8)]
    at_high = [lax.div(v, 4) * 32 for v in z_all]
    at_wall = [lax.rem(v, 4) for v in z_all]

    def target(d):
        return at_y[d[0]] + at_x[d[1]] + at_core[d[2]] + at_high[d[3]], at_wall[d[3]]

    order = deltas()
    barrier = pltpu.get_barrier_semaphore()
    for d in order:
        to_wide, to_wall = target(d)
        pl.semaphore_signal(
            barrier, inc=1, device_id={"wide": to_wide, "wall": to_wall}, device_id_type=MESH
        )

    def exchange(index, send, recv):
        mine = pl.ds(pl.multiple_of(slot * PIECE, PIECE), PIECE)
        own = pltpu.make_async_copy(send.at[mine], recv.at[mine], own_sem.at[index])
        own.start()
        for d in order:
            to_wide, to_wall = target(d)
            there = pl.multiple_of((to_wall * WIDE + to_wide) * PIECE, PIECE)
            pltpu.make_async_remote_copy(
                src_ref=send.at[pl.ds(there, PIECE)],
                dst_ref=recv.at[mine],
                send_sem=send_sem.at[index],
                recv_sem=recv_sem.at[index],
                device_id={"wide": to_wide, "wall": to_wall},
                device_id_type=MESH,
            ).start()
        own.wait()
        rest = pl.ds(0, (SLOTS - 1) * PIECE)
        pltpu.make_async_copy(send.at[rest], recv.at[rest], recv_sem.at[index]).wait()

    def sent(index, send, recv):
        rest = pl.ds(0, (SLOTS - 1) * PIECE)
        pltpu.make_async_copy(send.at[rest], recv.at[rest], send_sem.at[index]).wait()

    left, right = source[:, : X // 2], source[:, X // 2 :]
    for parity, half in enumerate((left + right, left - right)):
        rows = pl.ds(512 * parity, 512)
        send_a[rows, :] = dot3(stream_high[rows, :], stream_low[rows, :], half, NT)

    lanes = lax.broadcasted_iota(jnp.int32, (16, 128), 1)
    digit = lax.broadcasted_iota(jnp.int32, (16, 128), 0)
    upper_half = lanes >= 64
    kx = 2 * lax.rem(slot, 128) + lax.div(slot, 128) + jnp.where(upper_half, 256, 0)
    kz = 64 * digit + jnp.where(upper_half, lanes - 64, lanes)
    kz = jnp.where(kz < Z // 2, kz, kz - Z)
    stream_wave = kx.astype(jnp.float32) * (TWO_PI / X)
    span_wave = kz.astype(jnp.float32) * (TWO_PI / Z)
    wave_square = span_wave * span_wave + stream_wave * stream_wave
    widths = [jnp.full((16, 128), spacing[j], jnp.float32) for j in range(ROWS)]
    edges = (
        [2.0 / widths[0]]
        + [2.0 / (widths[j] + widths[j + 1]) for j in range(ROWS - 1)]
        + [2.0 / widths[ROWS - 1]]
    )
    previous = jnp.zeros((16, 128), jnp.float32)
    for j in range(ROWS):
        lower, upper = edges[j], edges[j + 1]
        inverse = 1.0 / (-(lower + upper) - wave_square * widths[j] - lower * previous)
        previous = upper * inverse
        pivot[j] = previous
        gain[j] = widths[j] * inverse
        carry[j] = lower * inverse
    weight = jnp.where(kx[:1] == 0, 1.0, 2.0) * (1.0 / (X * Z))

    pl.semaphore_wait(barrier, SLOTS - 1)
    exchange(0, send_a, recv_a)

    offset_re = jnp.zeros((16, 128), jnp.float32)
    offset_im = jnp.zeros((16, 128), jnp.float32)
    for block in range(WALL):
        rows = pl.ds(256 * block, 256)
        mixed = dot3(small_high[0:256, :], small_low[0:256, :], recv_a[rows, :], NN)
        re, im = mixed[:128], mixed[128:]
        cos, sin = twist[0], twist[1]
        turned = jnp.concatenate([re * cos + im * sin, im * cos - re * sin], axis=1)
        work[...] = dot3(small_high[256:512, :], small_low[256:512, :], turned, NT)
        for j in range(ROWS_HERE):
            row = block * ROWS_HERE + j
            offset_re = gain[row] * work[pl.ds(32 * j, 16), :] - carry[row] * offset_re
            offset_im = gain[row] * work[pl.ds(32 * j + 16, 16), :] - carry[row] * offset_im
            solved[pl.ds(32 * row, 16), :] = offset_re
            solved[pl.ds(32 * row + 16, 16), :] = offset_im
    value_re = offset_re
    value_im = offset_im
    for row in range(ROWS - 2, -1, -1):
        value_re = solved[pl.ds(32 * row, 16), :] - pivot[row] * value_re
        value_im = solved[pl.ds(32 * row + 16, 16), :] - pivot[row] * value_im
        solved[pl.ds(32 * row, 16), :] = value_re
        solved[pl.ds(32 * row + 16, 16), :] = value_im

    cos, sin = twist[2] * weight, twist[3] * weight
    for block in range(WALL):
        rows = pl.ds(256 * block, 256)
        mixed = dot3(small_high[512:768, :], small_low[512:768, :], solved[rows, :], NN)
        re, im = mixed[:128], mixed[128:]
        turned = jnp.concatenate([re * cos - im * sin, im * cos + re * sin], axis=1)
        send_b[rows, :] = dot3(small_high[768:1024, :], small_low[768:1024, :], turned, NT)

    exchange(1, send_b, recv_b)

    halves = []
    for parity in range(2):
        rows = pl.ds(512 * parity, 512)
        value = recv_b[rows, :].T
        value_high = value.astype(jnp.bfloat16)
        value_low = (value - value_high.astype(jnp.float32)).astype(jnp.bfloat16)
        dot = functools.partial(jnp.dot, preferred_element_type=jnp.float32)
        halves.append(
            dot(value_high, stream_high[rows, :])
            + (dot(value_low, stream_high[rows, :]) + dot(value_high, stream_low[rows, :]))
        )
    out[:, : X // 2] = halves[0] + halves[1]
    out[:, X // 2 :] = halves[0] - halves[1]
    sent(0, send_a, recv_a)
    sent(1, send_b, recv_b)


def shards(source, spacing):
    vmem = pl.BlockSpec(memory_space=pltpu.VMEM)
    plane = pltpu.VMEM((1024, 128), jnp.float32)
    coefficient = pltpu.VMEM((ROWS, 16, 128), jnp.float32)
    pressure = pl.pallas_call(
        kernel,
        out_shape=jax.ShapeDtypeStruct((ROWS_HERE * SPAN_HERE, X), jnp.float32),
        in_specs=[pl.BlockSpec(memory_space=pltpu.SMEM)] + [vmem] * 6,
        out_specs=vmem,
        scratch_shapes=[
            plane, plane, plane, plane, coefficient, coefficient, coefficient,
            pltpu.VMEM((256, 128), jnp.float32), plane,
            pltpu.SemaphoreType.DMA((2,)),
            pltpu.SemaphoreType.DMA((2,)),
            pltpu.SemaphoreType.DMA((2,)),
        ],
        compiler_params=pltpu.CompilerParams(
            collective_id=0, has_side_effects=True, vmem_limit_bytes=48 * 1024 * 1024
        ),
    )(spacing, source.reshape(ROWS_HERE * SPAN_HERE, X), *(jnp.asarray(t) for t in tables()))
    return pressure.reshape(source.shape)


def solution(mesh):
    in_specs = (P("wall", "wide", None), P())
    out_specs = P("wall", "wide", None)
    return jax.shard_map(shards, mesh=mesh, in_specs=in_specs, out_specs=out_specs, check_vma=False)
```

profile of v0, /device:TPU:1, one launch (start us, length us, event | category | flops | bytes accessed | tf_op | source)
XLA Modules:
  0.0 55.5 jit_solution(10553552906228800270)
XLA Ops:
  0.0 0.0 copy-start.6
  0.0 0.7 %copy-done.6 = f32[32]{0:T(128)S(1)} copy-done((f32[32]{0:T(128)S(1)}, f32[32]{0:T(128)}, u32[]{:S(2)}) %copy-start.6) | copy-done | bytes 152
  0.7 0.0 copy-start
  0.7 1.2 %copy-done = bf16[1024,512]{1,0:T(8,128)(2,1)S(1)} copy-done((bf16[1024,512]{1,0:T(8,128)(2,1)S(1)}, bf16[1024,512]{1,0:T(8,128)(2,1)}, u32[]{:S(2)}) %copy-start) | copy-done | bytes 1048600
  1.9 0.0 copy-start.1
  1.9 1.2 %copy-done.1 = bf16[1024,512]{1,0:T(8,128)(2,1)S(1)} copy-done((bf16[1024,512]{1,0:T(8,128)(2,1)S(1)}, bf16[1024,512]{1,0:T(8,128)(2,1)}, u32[]{:S(2)}) %copy-start.1) | copy-done | bytes 1048600
  3.1 0.0 copy-start.2
  3.1 1.0 %copy-done.2 = f32[8,16,1024]{2,1,0:T(8,128)S(1)} copy-done((f32[8,16,1024]{2,1,0:T(8,128)S(1)}, f32[8,16,1024]{2,1,0:T(8,128)}, u32[]{:S(2)}) %copy-start.2) | copy-done | bytes 524312
  4.1 0.0 copy-start.3
  4.2 1.0 %copy-done.3 = bf16[1024,256]{1,0:T(8,128)(2,1)S(1)} copy-done((bf16[1024,256]{1,0:T(8,128)(2,1)S(1)}, bf16[1024,256]{1,0:T(8,128)(2,1)}, u32[]{:S(2)}) %copy-start.3) | copy-done | bytes 524312
  5.2 0.0 copy-start.4
  5.2 1.0 %copy-done.4 = bf16[1024,256]{1,0:T(8,128)(2,1)S(1)} copy-done((bf16[1024,256]{1,0:T(8,128)(2,1)S(1)}, bf16[1024,256]{1,0:T(8,128)(2,1)}, u32[]{:S(2)}) %copy-start.4) | copy-done | bytes 524312
  6.2 0.0 copy-start.5
  6.2 0.9 %copy-done.5 = f32[4,128,128]{2,1,0:T(8,128)S(1)} copy-done((f32[4,128,128]{2,1,0:T(8,128)S(1)}, f32[4,128,128]{2,1,0:T(8,128)}, u32[]{:S(2)}) %copy-start.5) | copy-done | bytes 262168
  7.2 47.5 %shard_map.73 = f32[128,1024]{1,0:T(8,128)S(1)} custom-call(f32[32]{0:T(128)S(1)} %copy-done.6, f32[128,1024]{1,0:T(8,128)S(1)} %bitcast.3, bf16[1024,512]{1,0:T(8,128)(2,1)S(1)} %copy-done.1, bf16[1024,512]{1,0:T(8,128)(2,1)S(1)} %copy-done, bf16[1024,256]{1,0:T(8,128)(2,1)S(1)} %copy-done.4, bf16[1024,256]{1,0:T(8,128)(2,1)S(1)} %copy-done.3, ...), custom_call_target="tpu_custom_call" | custom-call | tf_op jit(solution)/shard_map/pallas_call | solution.py:224
  54.7 0.8 %copy.9 = f32[8,16,1024]{2,1,0:T(8,128)} copy(f32[8,16,1024]{2,1,0:T(8,128)S(1)} %bitcast.2) | data formatting | bytes 1048576
Async XLA Ops:
  0.0 0.7 %copy-start.6 = (f32[32]{0:T(128)S(1)}, f32[32]{0:T(128)}, u32[]{:S(2)}) copy-start(f32[32]{0:T(128)} %spacing.1) | copy-start | bytes 388
  0.7 1.2 %copy-start = (bf16[1024,512]{1,0:T(8,128)(2,1)S(1)}, bf16[1024,512]{1,0:T(8,128)(2,1)}, u32[]{:S(2)}) copy-start(bf16[1024,512]{1,0:T(8,128)(2,1)} %constant.11.clone.stream_low) | copy-start | bytes 3145732
  1.9 1.2 %copy-start.1 = (bf16[1024,512]{1,0:T(8,128)(2,1)S(1)}, bf16[1024,512]{1,0:T(8,128)(2,1)}, u32[]{:S(2)}) copy-start(bf16[1024,512]{1,0:T(8,128)(2,1)} %constant.10.clone.stream_high) | copy-start | bytes 3145732
  3.1 1.0 %copy-start.2 = (f32[8,16,1024]{2,1,0:T(8,128)S(1)}, f32[8,16,1024]{2,1,0:T(8,128)}, u32[]{:S(2)}) copy-start(f32[8,16,1024]{2,1,0:T(8,128)} %param.7) | copy-start | bytes 1572868
  4.1 1.0 %copy-start.3 = (bf16[1024,256]{1,0:T(8,128)(2,1)S(1)}, bf16[1024,256]{1,0:T(8,128)(2,1)}, u32[]{:S(2)}) copy-start(bf16[1024,256]{1,0:T(8,128)(2,1)} %constant.13.clone.small_low) | copy-start | bytes 1572868
  5.2 1.0 %copy-start.4 = (bf16[1024,256]{1,0:T(8,128)(2,1)S(1)}, bf16[1024,256]{1,0:T(8,128)(2,1)}, u32[]{:S(2)}) copy-start(bf16[1024,256]{1,0:T(8,128)(2,1)} %constant.12.clone.small_high) | copy-start | bytes 1572868
  6.2 0.9 %copy-start.5 = (f32[4,128,128]{2,1,0:T(8,128)S(1)}, f32[4,128,128]{2,1,0:T(8,128)}, u32[]{:S(2)}) copy-start(f32[4,128,128]{2,1,0:T(8,128)} %constant.14.clone.twist) | copy-start | bytes 786436
where the time goes:
time: 55.8 us; the launch traced here: 55.5 us
  Pallas kernels  47.5 us (85%)
  local copies, waits for them, and re-layouts  7.97 us (14%)
    pallas_call x1, Pallas kernels, shards(): pl.pallas_call(kernel, out_shape=jax.ShapeDtypeStruct((ROWS_HERE * SPAN_H...  47.5 us
    unnamed x15, local copies, waits for them, and re-layouts  7.97 us

commit v1 on v0

v1 whole, which is shorter than its diff:
```python
import functools
import math

import jax
import jax.numpy as jnp
import ml_dtypes
import numpy as np
from jax import lax
from jax.experimental import pallas as pl
from jax.experimental.pallas import tpu as pltpu
from jax.sharding import PartitionSpec as P

MESH = pl.DeviceIdType.MESH
TWO_PI = 2.0 * math.pi
X = 1024
Z = 1024
ROWS = 32
WALL = 4
WIDE = 64
SLOTS = WALL * WIDE
ROWS_HERE = ROWS // WALL
SPAN_HERE = Z // WIDE
PIECE = 2


def split_pair(table):
    high = table.astype(ml_dtypes.bfloat16)
    low = (table - high.astype(np.float64)).astype(ml_dtypes.bfloat16)
    return high, low


@functools.cache
def tables():
    x = np.arange(X // 2)
    slot = np.arange(SLOTS)
    mode = (2 * (slot % 128) + slot // 128)[None, :] + 256 * np.arange(2)[:, None]
    angle = TWO_PI * ((mode[..., None] * x) % X) / X
    stream = np.stack([np.cos(angle), -np.sin(angle)], axis=2).reshape(1024, 512)

    outer, inner = np.arange(64), np.arange(SPAN_HERE)
    angle = TWO_PI * ((outer[:, None] * outer[None, :]) % 64) / 64
    cos, sin = np.cos(angle), np.sin(angle)
    first = np.stack([np.stack([cos, sin], 2), np.stack([-sin, cos], 2)], 0)
    first = first.reshape(128, 128)
    angle = TWO_PI * ((inner[:, None] * inner[None, :]) % SPAN_HERE) / SPAN_HERE
    every_row = np.eye(ROWS_HERE)
    cos, sin = np.kron(every_row, np.cos(angle)), np.kron(every_row, np.sin(angle))
    angle = np.tile(TWO_PI * (outer[:, None] * inner[None, :]) / Z, (1, ROWS_HERE))
    turn_cos, turn_sin = np.cos(angle), np.sin(angle)
    twist = np.concatenate([turn_cos, turn_sin], axis=0)
    back_cos = np.concatenate([turn_cos.T, turn_cos.T], axis=1)
    back_sin = np.concatenate([-turn_sin.T, turn_sin.T], axis=1)
    small = np.concatenate(
        [first, first.T, cos, sin, twist, back_cos, back_sin], axis=1
    )
    small = np.pad(small, ((0, 0), (0, 128))).reshape(128, 2, 512).transpose(1, 0, 2).reshape(256, 512)
    return np.concatenate(split_pair(stream) + split_pair(small), axis=0)


def deltas():
    steps = [
        (y, x, core, z)
        for y in range(4)
        for x in range(4)
        for core in range(2)
        for z in range(8)
        if (y, x, core, z) != (0, 0, 0, 0)
    ]
    hops = lambda d: min(d[0], 4 - d[0]) + min(d[1], 4 - d[1])
    return sorted(steps, key=lambda d: (-hops(d), -min(d[3], 8 - d[3])))


def halves_of(value):
    high = value.astype(jnp.bfloat16)
    return high, (value - high.astype(jnp.float32)).astype(jnp.bfloat16)


def dot3(left, right, contract):
    dot = functools.partial(
        lax.dot_general,
        dimension_numbers=(contract, ((), ())),
        preferred_element_type=jnp.float32,
    )
    return dot(left[0], right[0]) + (dot(left[0], right[1]) + dot(left[1], right[0]))


NN = ((1,), (0,))
NT = ((1,), (1,))


def kernel(
    spacing_far, source_far, packed_far, out,
    spacing, source, packed,
    send_a, recv_a, send_b, recv_b, gain, carry, pivot, solved,
    send_sem, recv_sem, own_sem, load_sem,
):
    wide, wall = lax.axis_index("wide"), lax.axis_index("wall")
    slot = wall * WIDE + wide
    core = lax.rem(wide, 2)
    x = lax.rem(lax.div(wide, 2), 4)
    y = lax.rem(lax.div(wide, 8), 4)
    z = lax.div(wide, 32) * 4 + wall
    at_core = [lax.rem(core + d, 2) for d in range(2)]
    at_x = [lax.rem(x + d, 4) * 2 for d in range(4)]
    at_y = [lax.rem(y + d, 4) * 8 for d in range(4)]
    z_all = [lax.rem(z + d, 8) for d in range(8)]
    at_high = [lax.div(v, 4) * 32 for v in z_all]
    at_wall = [lax.rem(v, 4) for v in z_all]

    def target(d):
        return at_y[d[0]] + at_x[d[1]] + at_core[d[2]] + at_high[d[3]], at_wall[d[3]]

    order = deltas()
    barrier = pltpu.get_barrier_semaphore()
    for d in order:
        to_wide, to_wall = target(d)
        pl.semaphore_signal(
            barrier, inc=1, device_id={"wide": to_wide, "wall": to_wall}, device_id_type=MESH
        )
    loads = [
        pltpu.make_async_copy(there, here, load_sem.at[index])
        for index, (there, here) in enumerate(
            [
                (source_far, source),
                (packed_far.at[pl.ds(0, 2048)], packed.at[pl.ds(0, 2048)]),
                (spacing_far, spacing),
                (packed_far.at[pl.ds(2048, 512)], packed.at[pl.ds(2048, 512)]),
            ]
        )
    ]
    for load in loads:
        load.start()

    def start(index, k, send, recv):
        index = 2 * index + k
        mine = pl.ds(pl.multiple_of(k * 512 + slot * PIECE, PIECE), PIECE)
        pltpu.make_async_copy(send.at[mine], recv.at[mine], own_sem.at[index]).start()
        for d in order:
            to_wide, to_wall = target(d)
            there = pl.multiple_of(k * 512 + (to_wall * WIDE + to_wide) * PIECE, PIECE)
            pltpu.make_async_remote_copy(
                src_ref=send.at[pl.ds(there, PIECE)],
                dst_ref=recv.at[mine],
                send_sem=send_sem.at[index],
                recv_sem=recv_sem.at[index],
                device_id={"wide": to_wide, "wall": to_wall},
                device_id_type=MESH,
            ).start()

    def arrive(index, k, send, recv):
        index = 2 * index + k
        mine = pl.ds(pl.multiple_of(k * 512 + slot * PIECE, PIECE), PIECE)
        pltpu.make_async_copy(send.at[mine], recv.at[mine], own_sem.at[index]).wait()
        rest = pl.ds(k * 512, (SLOTS - 1) * PIECE)
        pltpu.make_async_copy(send.at[rest], recv.at[rest], recv_sem.at[index]).wait()

    def sent(index, k, send, recv):
        rest = pl.ds(k * 512, (SLOTS - 1) * PIECE)
        pltpu.make_async_copy(send.at[rest], recv.at[rest], send_sem.at[2 * index + k]).wait()

    loads[0].wait()
    loads[1].wait()
    left, right = source[:, : X // 2], source[:, X // 2 :]
    parts = halves_of(left + right), halves_of(left - right)

    def stream_rows(k, parity):
        base = 512 * k + 256 * parity
        return packed[pl.ds(base, 256), :], packed[pl.ds(1024 + base, 256), :]

    for k in range(2):
        for parity in range(2):
            rows = pl.ds(512 * k + 256 * parity, 256)
            send_a[rows, :] = dot3(stream_rows(k, parity), parts[parity], NT)

    loads[2].wait()
    lanes = lax.broadcasted_iota(jnp.int32, (16, 128), 1)
    digit = lax.broadcasted_iota(jnp.int32, (16, 128), 0)
    kz = 64 * digit + jnp.where(lanes >= 64, lanes - 64, lanes)
    kz = jnp.where(kz < Z // 2, kz, kz - Z)
    span_wave = kz.astype(jnp.float32) * (TWO_PI / Z)
    widths = [jnp.full((16, 128), spacing[j], jnp.float32) for j in range(ROWS)]
    edges = (
        [2.0 / widths[0]]
        + [2.0 / (widths[j] + widths[j + 1]) for j in range(ROWS - 1)]
        + [2.0 / widths[ROWS - 1]]
    )
    first_mode = 2 * lax.rem(slot, 128) + lax.div(slot, 128)
    wave_square, previous = [], []
    for k in range(2):
        kx = jnp.full((16, 128), first_mode + 256 * k, jnp.int32)
        stream_wave = kx.astype(jnp.float32) * (TWO_PI / X)
        wave_square.append(span_wave * span_wave + stream_wave * stream_wave)
        previous.append(jnp.zeros((16, 128), jnp.float32))
    for j in range(ROWS):
        lower, upper = edges[j], edges[j + 1]
        for k in range(2):
            divisor = -(lower + upper) - wave_square[k] * widths[j] - lower * previous[k]
            inverse = 1.0 / divisor
            previous[k] = upper * inverse
            pivot[k, j] = previous[k]
            gain[k, j] = widths[j] * inverse
            carry[k, j] = lower * inverse

    loads[3].wait()

    def table(index):
        high, columns = 2048 + 128 * (index // 4), pl.ds(128 * (index % 4), 128)
        return packed[pl.ds(high, 128), columns], packed[pl.ds(high + 256, 128), columns]

    def number(index):
        high, low = table(index)
        return high.astype(jnp.float32) + low.astype(jnp.float32)

    pl.semaphore_wait(barrier, SLOTS - 1)
    start(0, 0, send_a, recv_a)
    start(0, 1, send_a, recv_a)

    for k in range(2):
        arrive(0, k, send_a, recv_a)
        twist = number(4)
        cos, sin = twist[:64], twist[64:]
        wave_cos, wave_sin = table(2), table(3)
        second = tuple(jnp.concatenate([c, s], axis=1) for c, s in zip(wave_cos, wave_sin))
        offset = jnp.zeros((16, 128), jnp.float32)
        for block in range(WALL):
            rows = pl.ds(512 * k + 128 * block, 128)
            mixed = dot3(table(0), halves_of(recv_a[rows, :]), NN)
            re, im = mixed[:64], mixed[64:]
            turned_re = halves_of(re * cos + im * sin)
            turned_im = halves_of(im * cos - re * sin)
            turned = tuple(
                jnp.concatenate(
                    [jnp.concatenate([r, i], axis=1), jnp.concatenate([i, -r], axis=1)], axis=0
                )
                for r, i in zip(turned_re, turned_im)
            )
            work = dot3(second, turned, NT)
            for j in range(ROWS_HERE):
                row = block * ROWS_HERE + j
                offset = gain[k, row] * work[16 * j : 16 * j + 16] - carry[k, row] * offset
                solved[pl.ds(16 * row, 16), :] = offset
        value = offset
        for row in range(ROWS - 2, -1, -1):
            value = solved[pl.ds(16 * row, 16), :] - pivot[k, row] * value
            solved[pl.ds(16 * row, 16), :] = value

        weight = 1.0 / (X * Z)
        kx = jnp.full((1, 128), first_mode + 256 * k, jnp.int32)
        weight = jnp.where(kx == 0, weight, 2.0 * weight)
        cos, sin = number(5) * weight, number(6) * weight
        sign = jnp.where(lanes[:1] < 64, -1.0, 1.0)
        for block in range(WALL):
            rows = pl.ds(512 * k + 128 * block, 128)
            value = halves_of(solved[pl.ds(128 * block, 128), :])
            mixed = dot3(wave_cos, value, NN) + sign * pltpu.roll(dot3(wave_sin, value, NN), 64, 1)
            turned = halves_of(mixed * cos + pltpu.roll(mixed, 64, 1) * sin)
            send_b[rows, :] = dot3(table(1), turned, NT)
        start(1, k, send_b, recv_b)

    sums = [0.0, 0.0]
    for k in range(2):
        arrive(1, k, send_b, recv_b)
        for parity in range(2):
            rows = pl.ds(512 * k + 256 * parity, 256)
            sums[parity] += dot3(halves_of(recv_b[rows, :].T), stream_rows(k, parity), NN)
    out[:, : X // 2] = sums[0] + sums[1]
    out[:, X // 2 :] = sums[0] - sums[1]
    for k in range(2):
        sent(0, k, send_a, recv_a)
        sent(1, k, send_b, recv_b)


def shards(source, spacing):
    plane = pltpu.VMEM((1024, 128), jnp.float32)
    coefficient = pltpu.VMEM((2, ROWS, 16, 128), jnp.float32)
    semaphores = pltpu.SemaphoreType.DMA((4,))
    pressure = pl.pallas_call(
        kernel,
        out_shape=jax.ShapeDtypeStruct((ROWS_HERE * SPAN_HERE, X), jnp.float32),
        in_specs=[pl.BlockSpec(memory_space=pl.ANY)] * 3,
        out_specs=pl.BlockSpec(memory_space=pltpu.VMEM),
        scratch_shapes=[
            pltpu.SMEM((ROWS,), jnp.float32),
            pltpu.VMEM((ROWS_HERE * SPAN_HERE, X), jnp.float32),
            pltpu.VMEM((2560, 512), jnp.bfloat16),
            plane, plane, plane, plane, coefficient, coefficient, coefficient,
            pltpu.VMEM((512, 128), jnp.float32),
            semaphores, semaphores, semaphores, semaphores,
        ],
        compiler_params=pltpu.CompilerParams(
            collective_id=0, has_side_effects=True, vmem_limit_bytes=53 * 1024 * 1024
        ),
    )(spacing, source.reshape(ROWS_HERE * SPAN_HERE, X), jnp.asarray(tables()))
    return pressure.reshape(source.shape)


def solution(mesh):
    in_specs = (P("wall", "wide", None), P())
    out_specs = P("wall", "wide", None)
    return jax.shard_map(shards, mesh=mesh, in_specs=in_specs, out_specs=out_specs, check_vma=False)
```

time: 55.8 us -> 42.6 us (0.76)
  local copies, waits for them, and re-layouts: 7.97 us -> 1.45 us
  Pallas kernels: 47.5 us -> 41 us
    unnamed x15 -> x3, local copies, waits for them, and re-layouts: 7.97 us -> 1.45 us
    pallas_call x1, Pallas kernels: 47.5 us -> 41 us  [shards(): pl.pallas_call(kernel, out_shape=jax.ShapeDtypeStruct((ROWS_HERE * SPAN_H...]
where the time goes in v1:
time: 42.6 us; the launch traced here: 42.5 us
  Pallas kernels  41 us (96%)
  local copies, waits for them, and re-layouts  1.45 us (3%)
    pallas_call x1, Pallas kernels, shards(): pl.pallas_call(kernel, out_shape=jax.ShapeDtypeStruct((ROWS_HERE * SPAN_H...  41 us
    unnamed x3, local copies, waits for them, and re-layouts  1.45 us

profile of v1, /device:TPU:1, one launch (start us, length us, event | category | flops | bytes accessed | tf_op | source)
XLA Modules:
  0.0 42.5 jit_solution(773368021091030928)
XLA Ops:
  0.0 0.0 copy-start
  0.0 0.7 %copy-done = f32[32]{0:T(128)S(1)} copy-done((f32[32]{0:T(128)S(1)}, f32[32]{0:T(128)}, u32[]{:S(2)}) %copy-start) | copy-done | bytes 152
  0.7 41.0 %shard_map.37 = f32[128,1024]{1,0:T(8,128)S(1)} custom-call(f32[32]{0:T(128)S(1)} %copy-done, f32[128,1024]{1,0:T(8,128)} %bitcast.3, bf16[2560,512]{1,0:T(8,128)(2,1)} %constant.2.clone.packed_far), custom_call_target="tpu_custom_call" | custom-call | tf_op jit(solution)/shard_map/pallas_call | solution.py:277
  41.7 0.8 %copy.5 = f32[8,16,1024]{2,1,0:T(8,128)} copy(f32[8,16,1024]{2,1,0:T(8,128)S(1)} %bitcast.2) | data formatting | bytes 1048576
Async XLA Ops:
  0.0 0.7 %copy-start = (f32[32]{0:T(128)S(1)}, f32[32]{0:T(128)}, u32[]{:S(2)}) copy-start(f32[32]{0:T(128)} %spacing_far.1) | copy-start | bytes 388

commit v2 on v1

--- a/solution.py
+++ b/solution.py
@@ -57,7 +57,7 @@
     return np.concatenate(split_pair(stream) + split_pair(small), axis=0)
 
 
-def deltas():
+def deltas(spanwise_first):
     steps = [
         (y, x, core, z)
         for y in range(4)
@@ -66,8 +66,11 @@
         for z in range(8)
         if (y, x, core, z) != (0, 0, 0, 0)
     ]
-    hops = lambda d: min(d[0], 4 - d[0]) + min(d[1], 4 - d[1])
-    return sorted(steps, key=lambda d: (-hops(d), -min(d[3], 8 - d[3])))
+    across = lambda d: min(d[0], 4 - d[0]) + min(d[1], 4 - d[1])
+    along = lambda d: min(d[3], 8 - d[3])
+    if spanwise_first:
+        return sorted(steps, key=lambda d: -along(d) - across(d))
+    return sorted(steps, key=lambda d: (-across(d), -along(d)))
 
 
 def halves_of(value):
@@ -110,26 +113,29 @@
     def target(d):
         return at_y[d[0]] + at_x[d[1]] + at_core[d[2]] + at_high[d[3]], at_wall[d[3]]
 
-    order = deltas()
-    barrier = pltpu.get_barrier_semaphore()
-    for d in order:
-        to_wide, to_wall = target(d)
-        pl.semaphore_signal(
-            barrier, inc=1, device_id={"wide": to_wide, "wall": to_wall}, device_id_type=MESH
-        )
     loads = [
         pltpu.make_async_copy(there, here, load_sem.at[index])
         for index, (there, here) in enumerate(
             [
                 (source_far, source),
-                (packed_far.at[pl.ds(0, 2048)], packed.at[pl.ds(0, 2048)]),
+                (packed_far.at[pl.ds(0, 512)], packed.at[pl.ds(0, 512)]),
+                (packed_far.at[pl.ds(1024, 512)], packed.at[pl.ds(1024, 512)]),
+                (packed_far.at[pl.ds(512, 512)], packed.at[pl.ds(512, 512)]),
+                (packed_far.at[pl.ds(1536, 512)], packed.at[pl.ds(1536, 512)]),
+                (packed_far.at[pl.ds(2048, 512)], packed.at[pl.ds(2048, 512)]),
                 (spacing_far, spacing),
-                (packed_far.at[pl.ds(2048, 512)], packed.at[pl.ds(2048, 512)]),
             ]
         )
     ]
     for load in loads:
         load.start()
+    barrier = pltpu.get_barrier_semaphore()
+    for d in deltas(True):
+        to_wide, to_wall = target(d)
+        pl.semaphore_signal(
+            barrier, inc=1, device_id={"wide": to_wide, "wall": to_wall}, device_id_type=MESH
+        )
+    order = deltas(False)
 
     def start(index, k, send, recv):
         index = 2 * index + k
@@ -158,8 +164,8 @@
         rest = pl.ds(k * 512, (SLOTS - 1) * PIECE)
         pltpu.make_async_copy(send.at[rest], recv.at[rest], send_sem.at[2 * index + k]).wait()
 
-    loads[0].wait()
-    loads[1].wait()
+    for load in loads[:3]:
+        load.wait()
     left, right = source[:, : X // 2], source[:, X // 2 :]
     parts = halves_of(left + right), halves_of(left - right)
 
@@ -167,12 +173,19 @@
         base = 512 * k + 256 * parity
         return packed[pl.ds(base, 256), :], packed[pl.ds(1024 + base, 256), :]
 
-    for k in range(2):
+    def transform(k):
         for parity in range(2):
             rows = pl.ds(512 * k + 256 * parity, 256)
             send_a[rows, :] = dot3(stream_rows(k, parity), parts[parity], NT)
 
-    loads[2].wait()
+    transform(0)
+    pl.semaphore_wait(barrier, SLOTS - 1)
+    start(0, 0, send_a, recv_a)
+    for load in loads[3:]:
+        load.wait()
+    transform(1)
+    start(0, 1, send_a, recv_a)
+
     lanes = lax.broadcasted_iota(jnp.int32, (16, 128), 1)
     digit = lax.broadcasted_iota(jnp.int32, (16, 128), 0)
     kz = 64 * digit + jnp.where(lanes >= 64, lanes - 64, lanes)
@@ -201,8 +214,6 @@
             gain[k, j] = widths[j] * inverse
             carry[k, j] = lower * inverse
 
-    loads[3].wait()
-
     def table(index):
         high, columns = 2048 + 128 * (index // 4), pl.ds(128 * (index % 4), 128)
         return packed[pl.ds(high, 128), columns], packed[pl.ds(high + 256, 128), columns]
@@ -210,10 +221,6 @@
     def number(index):
         high, low = table(index)
         return high.astype(jnp.float32) + low.astype(jnp.float32)
-
-    pl.semaphore_wait(barrier, SLOTS - 1)
-    start(0, 0, send_a, recv_a)
-    start(0, 1, send_a, recv_a)
 
     for k in range(2):
         arrive(0, k, send_a, recv_a)
@@ -276,7 +283,7 @@
     semaphores = pltpu.SemaphoreType.DMA((4,))
     pressure = pl.pallas_call(
         kernel,
-        out_shape=jax.ShapeDtypeStruct((ROWS_HERE * SPAN_HERE, X), jnp.float32),
+        out_shape=pltpu.VMEM((ROWS_HERE * SPAN_HERE, X), jnp.float32),
         in_specs=[pl.BlockSpec(memory_space=pl.ANY)] * 3,
         out_specs=pl.BlockSpec(memory_space=pltpu.VMEM),
         scratch_shapes=[
@@ -285,12 +292,16 @@
             pltpu.VMEM((2560, 512), jnp.bfloat16),
             plane, plane, plane, plane, coefficient, coefficient, coefficient,
             pltpu.VMEM((512, 128), jnp.float32),
-            semaphores, semaphores, semaphores, semaphores,
+            semaphores, semaphores, semaphores, pltpu.SemaphoreType.DMA((7,)),
         ],
         compiler_params=pltpu.CompilerParams(
-            collective_id=0, has_side_effects=True, vmem_limit_bytes=53 * 1024 * 1024
+            collective_id=0, has_side_effects=True, vmem_limit_bytes=32 * 1024 * 1024
         ),
-    )(spacing, source.reshape(ROWS_HERE * SPAN_HERE, X), jnp.asarray(tables()))
+    )(
+        pltpu.with_memory_space_constraint(spacing, pltpu.HBM),
+        pltpu.with_memory_space_constraint(source.reshape(ROWS_HERE * SPAN_HERE, X), pltpu.HBM),
+        pltpu.with_memory_space_constraint(jnp.asarray(tables()), pltpu.HBM),
+    )
     return pressure.reshape(source.shape)
 
 

time: 42.6 us -> 41.9 us (0.984)
  local copies, waits for them, and re-layouts: 1.45 us -> 0.8 us
    unnamed x3 -> x1, local copies, waits for them, and re-layouts: 1.45 us -> 0.8 us
where the time goes in v2:
time: 41.9 us; the launch traced here: 41.8 us
  Pallas kernels  41 us (98%)
  local copies, waits for them, and re-layouts  0.8 us (2%)
    pallas_call x1, Pallas kernels, shards(): pl.pallas_call(kernel, out_shape=pltpu.VMEM((ROWS_HERE * SPAN_HERE, X), j...  41 us

profile of v2, /device:TPU:1, one launch (start us, length us, event | category | flops | bytes accessed | tf_op | source)
XLA Modules:
  0.0 41.8 jit_solution(14914546987201291709)
XLA Ops:
  0.0 41.0 %shard_map.37 = f32[128,1024]{1,0:T(8,128)S(1)} custom-call(f32[32]{0:T(128)} %spacing_far.1, f32[128,1024]{1,0:T(8,128)} %bitcast.3, bf16[2560,512]{1,0:T(8,128)(2,1)} %constant.2.clone.packed_far), custom_call_target="tpu_custom_call" | custom-call | tf_op jit(solution)/shard_map/pallas_call | solution.py:284
  41.0 0.8 %copy.5 = f32[8,16,1024]{2,1,0:T(8,128)} copy(f32[8,16,1024]{2,1,0:T(8,128)S(1)} %bitcast.2) | data formatting | bytes 1048576

commit v3 on v2

--- a/solution.py
+++ b/solution.py
@@ -127,10 +127,11 @@
             ]
         )
     ]
-    for load in loads:
-        load.start()
     barrier = pltpu.get_barrier_semaphore()
-    for d in deltas(True):
+    for position, d in enumerate(deltas(True)):
+        if position == 32:
+            for load in loads:
+                load.start()
         to_wide, to_wall = target(d)
         pl.semaphore_signal(
             barrier, inc=1, device_id={"wide": to_wide, "wall": to_wall}, device_id_type=MESH

time: 41.9 us -> 41.9 us (level)
  no operation moved by 1% of the time
where the time goes in v3:
time: 41.9 us; the launch traced here: 41.8 us
  Pallas kernels  41 us (98%)
  local copies, waits for them, and re-layouts  0.8 us (2%)
    pallas_call x1, Pallas kernels, shards(): pl.pallas_call(kernel, out_shape=pltpu.VMEM((ROWS_HERE * SPAN_HERE, X), j...  41 us

profile of v3, /device:TPU:1, one launch (start us, length us, event | category | flops | bytes accessed | tf_op | source)
XLA Modules:
  0.0 41.8 jit_solution(11978690251921125694)
XLA Ops:
  0.0 41.0 %shard_map.37 = f32[128,1024]{1,0:T(8,128)S(1)} custom-call(f32[32]{0:T(128)} %spacing_far.1, f32[128,1024]{1,0:T(8,128)} %bitcast.3, bf16[2560,512]{1,0:T(8,128)(2,1)} %constant.2.clone.packed_far), custom_call_target="tpu_custom_call" | custom-call | tf_op jit(solution)/shard_map/pallas_call | solution.py:285
  41.0 0.8 %copy.5 = f32[8,16,1024]{2,1,0:T(8,128)} copy(f32[8,16,1024]{2,1,0:T(8,128)S(1)} %bitcast.2) | data formatting | bytes 1048576
